TPU v7x, 32 devices: a whole 2x2x4 slice. The times are simulated.
32 devices in a mesh: dp: 4 (over y, x), row: 2 (over core), col: 4 (over z).
Axes of the slice: x: 2, y: 2, z: 4, core: 2. Of those that a mesh axis runs over, the one named last changes fastest.
Arguments:
- pixels: bfloat16 [4, 64, 384, 256], P('dp', 'row', 'col'), may hold values from -6 to 6
- hidden_pre: bfloat16 [4, 32, 192, 256], P('dp', 'row', 'col'), may hold values from -6 to 6
- upstream: bfloat16 [4, 16, 96, 512], P('dp', 'row', 'col'), may hold values from -6 to 6
- kernel_first: bfloat16 [3, 3, 256, 256], replicated, may hold values from -0.125 to 0.125
- kernel_second: bfloat16 [3, 3, 256, 512], replicated, may hold values from -0.125 to 0.125
Outputs:
- grad_pixels: bfloat16 [4, 64, 384, 256], P('dp', 'row', 'col')
- grad_kernel_first: float32 [2304, 256], P(('row', 'col'))
- grad_kernel_second: float32 [2304, 512], P(('row', 'col'))
All inputs are finite; a program needn't handle non-finite values.
Results may differ from a plain program's by a relative error of at most 0.0049.
Values may be sent and summed in bfloat16 or wider, within the bound.
A program may use at most 64 MiB of HBM per device.

v0:
```python
import math
import jax
import jax.numpy as jnp
from jax import lax
from jax.sharding import PartitionSpec as P


def shifted(value, axis, by):
    peers = lax.axis_size(axis)
    pairs = [(i, i + by) for i in range(peers) if 0 <= i + by < peers]
    return lax.ppermute(value, axis, pairs)


def extend_field(tile_field):
    from_above = shifted(tile_field[-1], "row", 1)
    from_left = shifted(tile_field[:, -1], "col", 1)
    corner = shifted(from_left[-1:], "row", 1)
    top_row = jnp.concatenate([corner, from_above], axis=0)
    lower_rows = jnp.concatenate([from_left[:, None], tile_field], axis=1)
    return jnp.concatenate([top_row[None], lower_rows], axis=0)


def gather_taps(extended, out_rows, out_cols):
    tap_list = []
    for tap_row in range(3):
        for tap_col in range(3):
            tap_list.append(
                extended[tap_row : tap_row + 2 * out_rows : 2, tap_col : tap_col + 2 * out_cols : 2]
            )
    stacked = jnp.concatenate(tap_list, axis=-1)
    return stacked.reshape(out_rows * out_cols, stacked.shape[-1])


def spread_taps(tap_terms):
    row_count = tap_terms.shape[0]
    col_count = tap_terms.shape[1]
    channels = tap_terms.shape[-1]
    even_part = jnp.pad(tap_terms[:, :, 0], ((0, 1), (0, 0), (0, 0), (0, 0))) + jnp.pad(
        tap_terms[:, :, 2], ((1, 0), (0, 0), (0, 0), (0, 0))
    )
    odd_part = jnp.pad(tap_terms[:, :, 1], ((0, 1), (0, 0), (0, 0), (0, 0)))
    merged = jnp.stack([even_part, odd_part], axis=1).reshape(
        2 * row_count + 2, col_count, 3, channels
    )[: 2 * row_count + 1]
    even_part = jnp.pad(merged[:, :, 0], ((0, 0), (0, 1), (0, 0))) + jnp.pad(
        merged[:, :, 2], ((0, 0), (1, 0), (0, 0))
    )
    odd_part = jnp.pad(merged[:, :, 1], ((0, 0), (0, 1), (0, 0)))
    return jnp.stack([even_part, odd_part], axis=2).reshape(
        2 * row_count + 1, 2 * col_count + 2, channels
    )[:, : 2 * col_count + 1]


def settle_edges(padded):
    interior = padded[1:, 1:]
    from_below = shifted(padded[0, 1:], "row", -1)
    from_right = shifted(padded[:, 0], "col", -1)
    corner = shifted(from_right[:1], "row", -1)
    from_below = from_below.at[-1].add(corner[0])
    interior = interior.at[:, -1].add(from_right[1:])
    return interior.at[-1].add(from_below)


def kernel_gradient(patches, gradient, norm_scale):
    slide_sums = lax.psum(
        lax.dot_general(
            patches, gradient, (((0,), (0,)), ((), ())), preferred_element_type=jnp.float32
        )
        * norm_scale,
        "dp",
    )
    return lax.psum_scatter(slide_sums, ("row", "col"), scatter_dimension=0, tiled=True)


def per_device(pixels, hidden_pre, upstream, kernel_first, kernel_second):
    source = pixels[0]
    hidden = hidden_pre[0]
    cotangent_tile = upstream[0]
    rows_two, cols_two, width_two = cotangent_tile.shape
    rows_one, cols_one, width_one = hidden.shape
    width_zero = source.shape[-1]
    devices_all = lax.axis_size("dp") * lax.axis_size("row") * lax.axis_size("col")
    scale_one = 1.0 / math.sqrt(devices_all * rows_one * cols_one)
    scale_two = 1.0 / math.sqrt(devices_all * rows_two * cols_two)
    flat_second = kernel_second.reshape(9 * width_one, width_two)
    flat_first = kernel_first.reshape(9 * width_zero, width_one)
    cotangent = cotangent_tile.reshape(rows_two * cols_two, width_two)
    terms_two = lax.dot_general(
        cotangent, flat_second, (((1,), (1,)), ((), ())), preferred_element_type=jnp.float32
    )
    grad_active = settle_edges(spread_taps(terms_two.reshape(rows_two, cols_two, 3, 3, width_one)))
    active = jnp.maximum(hidden, 0)
    active_patches = gather_taps(extend_field(active), rows_two, cols_two)
    grad_kernel_second = kernel_gradient(active_patches, cotangent, scale_two)
    grad_pre = jnp.where(hidden > 0, grad_active, 0.0).astype(jnp.bfloat16)
    grad_rows = grad_pre.reshape(rows_one * cols_one, width_one)
    terms_one = lax.dot_general(
        grad_rows, flat_first, (((1,), (1,)), ((), ())), preferred_element_type=jnp.float32
    )
    grad_source = settle_edges(
        spread_taps(terms_one.reshape(rows_one, cols_one, 3, 3, width_zero))
    ).astype(jnp.bfloat16)
    source_patches = gather_taps(extend_field(source), rows_one, cols_one)
    grad_kernel_first = kernel_gradient(source_patches, grad_rows, scale_one)
    return (grad_source[None], grad_kernel_first, grad_kernel_second)


def solution(mesh):
    in_specs = (
        P("dp", "row", "col", None),
        P("dp", "row", "col", None),
        P("dp", "row", "col", None),
        P(),
        P(),
    )
    out_specs = (P("dp", "row", "col", None), P(("row", "col"), None), P(("row", "col"), None))
    return jax.shard_map(
        per_device, mesh=mesh, in_specs=in_specs, out_specs=out_specs, check_vma=False
    )
```

profile of v0, /device:TPU:0, one launch (start us, length us, event | category | flops | bytes accessed | tf_op | source)
XLA Modules:
  0.0 331.8 jit_solution(14036254897099947175)
XLA Ops:
  7.2 1.6 copy-done
  8.8 1.8 fusion.1
  11.6 1.6 copy.44
  13.2 1.8 reshape.226
  15.6 1.3 collective-permute-start
  16.9 0.6 slice_bitcast_fusion.13
  17.5 1.3 collective-permute-start.1
  19.5 6.1 %collective-permute-start.6 = (bf16[32,256]{1,0:T(8,128)(2,1)}, bf16[32,256]{1,0:T(8,128)(2,1)}, u32[]{:S(2)}, u32[]{:S(2)}) collective-permute-start(bf16[32,256]{1,0:T(8,128)(2,1)} %bitcast.134), channel_id=1, source_target_pairs={{0,1},{1,2},{2,3},{4,5},{5,6},{6,7},{8,9},{9,10},{10,11},{12,13},{... | collective-permute-start | bytes 49160 | tf_op jit(solution)/shard_map/ppermute | solution.py:11
  26.2 4.0 %collective-permute-start.8 = (bf16[96,256]{1,0:T(8,128)(2,1)}, bf16[96,256]{1,0:T(8,128)(2,1)}, u32[]{:S(2)}, u32[]{:S(2)}) collective-permute-start(bf16[96,256]{1,0:T(8,128)(2,1)} %slice_bitcast_fusion.14), channel_id=1, source_target_pairs={{0,4},{1,5},{2,6},{3,7},{8,12},{9,13},{10,14},{11,15},{16,20},{17,... | collective-permute-start | bytes 147464 | tf_op jit(solution)/shard_map/ppermute | solution.py:11
  30.3 5.1 %slice.315 = bf16[16,48,256]{2,1,0:T(8,128)(2,1)} slice(bf16[32,96,256]{2,1,0:T(8,128)(2,1)S(1)} %bitcast.138), slice={[0:32:2], [0:96:2], [0:256:1]} | slice | bytes 786432 | tf_op jit(solution)/shard_map/slice | solution.py:28
  35.4 0.7 slice.316
  36.1 1.0 slice.318
  37.2 1.0 slice.319
  38.2 0.7 copy.58
  39.6 2.1 pad_maximum_fusion.2
  41.7 9.2 %slice.314 = bf16[16,48,256]{2,1,0:T(8,128)(2,1)} slice(bf16[32,97,256]{2,1,0:T(8,128)(2,1)} %pad_maximum_fusion.2), slice={[0:32:2], [0:96:2], [0:256:1]} | slice | bytes 786432 | tf_op jit(solution)/shard_map/slice | solution.py:28
  50.9 9.1 %slice.317 = bf16[16,48,256]{2,1,0:T(8,128)(2,1)} slice(bf16[32,97,256]{2,1,0:T(8,128)(2,1)} %pad_maximum_fusion.2), slice={[1:32:2], [0:96:2], [0:256:1]} | slice | bytes 786432 | tf_op jit(solution)/shard_map/slice | solution.py:28
  60.0 1.3 slice.361
  61.2 1.8 collective-permute-start.7
  63.1 0.7 fusion.10
  63.8 1.3 slice.345
  65.1 1.3 collective-permute-start.2
  66.5 0.8 maximum_bitcast_fusion
  67.3 3.0 maximum_maximum_fusion
  70.4 7.6 %slice.311 = bf16[16,48,256]{2,1,0:T(8,128)(2,1)S(1)} slice(bf16[33,97,256]{2,1,0:T(8,128)(2,1)} %maximum_maximum_fusion), slice={[0:32:2], [0:96:2], [0:256:1]} | slice | bytes 786432 | tf_op jit(solution)/shard_map/slice | solution.py:28
  78.0 0.8 constant_dynamic-update-slice_fusion.8
  78.8 9.2 %slice.312 = bf16[16,48,256]{2,1,0:T(8,128)(2,1)} slice(bf16[33,97,256]{2,1,0:T(8,128)(2,1)} %maximum_maximum_fusion), slice={[0:32:2], [1:97:2], [0:256:1]} | slice | bytes 786432 | tf_op jit(solution)/shard_map/slice | solution.py:28
  88.0 7.6 %slice.313 = bf16[16,48,256]{2,1,0:T(8,128)(2,1)S(1)} slice(bf16[33,97,256]{2,1,0:T(8,128)(2,1)} %maximum_maximum_fusion), slice={[0:32:2], [2:97:2], [0:256:1]} | slice | bytes 786432 | tf_op jit(solution)/shard_map/slice | solution.py:28
  95.6 0.7 fusion.12
  96.4 1.3 scatter-add.21
  97.7 0.8 fusion.8
  98.5 1.8 constant_dynamic-update-slice_fusion.7
  100.3 0.8 constant_dynamic-update-slice_fusion.6
  101.1 0.8 constant_dynamic-update-slice_fusion.5
  101.9 0.9 constant_dynamic-update-slice_fusion.4
  102.7 0.8 constant_dynamic-update-slice_fusion.3
  103.6 0.8 constant_dynamic-update-slice_fusion.2
  104.4 0.8 constant_dynamic-update-slice_fusion.1
  105.2 0.8 constant_dynamic-update-slice_fusion
  106.0 4.6 %fusion = f32[2304,256]{1,0:T(8,128)} fusion(bf16[16,48,2304]{2,1,0:T(8,128)(2,1)} %constant_dynamic-update-slice_fusion, f32[16,48,256]{2,1,0:T(8,128)S(1)} %fusion.8, bf16[1,16,48,256]{3,2,1,0:T(8,128)(2,1)S(1)} %copy-done.3), kind=kOutput, calls=%fused_computation.3 | convolution fusion | flops 907345920 | bytes 7077888 | tf_op jit(solution)/shard_map/dot_general | solution.py:66
  110.8 3.3 %collective-permute-start.9 = (bf16[16,256]{1,0:T(8,128)(2,1)S(1)}, bf16[16,256]{1,0:T(8,128)(2,1)S(1)}, u32[]{:S(2)}, u32[]{:S(2)}) collective-permute-start(bf16[16,256]{1,0:T(8,128)(2,1)S(1)} %bitcast.150), channel_id=1, source_target_pairs={{0,1},{1,2},{2,3},{4,5},{5,6},{6,7},{8,9},{9,10},{10,11},{12,13},{... | collective-permute-start | bytes 24584 | tf_op jit(solution)/shard_map/ppermute | solution.py:11
  114.2 3.3 collective-permute-start.11
  119.0 1.3 collective-permute-start.10
  122.4 3.0 convolution_multiply_fusion
  125.6 1.0 copy-done.7
  126.7 1.1 fusion.3
  127.8 0.7 slice_bitcast_fusion.2
  131.3 3.4 %copy.53 = f32[33,49,2,256]{3,2,1,0:T(2,128)} copy(f32[33,49,2,256]{3,1,0,2:T(8,128)S(1)} %pad_maximum_fusion.1) | data formatting | bytes 6623232 | tf_op jit(solution)/shard_map/stack | solution.py:49
  134.7 4.0 %reshape.231 = f32[33,98,256]{2,1,0:T(8,128)S(1)} reshape(f32[33,49,2,256]{3,2,1,0:T(2,128)} %copy.53) | data formatting | bytes 6623232 | tf_op jit(solution)/shard_map/reshape | solution.py:49
  138.8 1.3 collective-permute-start.3
  140.1 0.7 slice_bitcast_fusion.12
  140.8 2.1 slice.352
  142.9 1.3 collective-permute-start.4
  144.2 2.7 collective-permute-done.3
  147.6 1.3 collective-permute-start.5
  148.8 18.9 %reduce-scatter.3.cloned.1.call-done = f32[288,256]{1,0:T(8,128)} async-done(((f32[2304,256]{1,0:T(8,128)}), f32[288,256]{1,0:T(8,128)}) %reduce-scatter.3.cloned.1.call-update) | async-done | bytes 294928 | tf_op jit(solution)/shard_map/reduce_scatter | solution.py:72
  167.7 100.3 %reduce-scatter.5.cloned.1.call-done = f32[288,512]{1,0:T(8,128)} async-done(((f32[2304,512]{1,0:T(8,128)}), f32[288,512]{1,0:T(8,128)}) %reduce-scatter.5.cloned.1.call-update) | async-done | bytes 589840 | tf_op jit(solution)/shard_map/reduce_scatter | solution.py:72
  268.1 0.8 fusion.9
  268.9 1.8 scatter-add.25
  270.7 1.7 fusion.7
  272.4 3.3 convert_bitcast_fusion
  275.7 45.9 %all-reduce.15.cloned.1.call-done = (f32[288,256]{1,0:T(8,128)}, f32[288,512]{1,0:T(8,128)}) async-done(((f32[288,256]{1,0:T(8,128)}, f32[288,512]{1,0:T(8,128)}), (f32[288,256]{1,0:T(8,128)}, f32[288,512]{1,0:T(8,128)})) %all-reduce.15.cloned.1.call-update) | async-done | bytes 884752 | tf_op jit(solution)/shard_map/psum | solution.py:65
  321.6 1.7 copy.111
  323.3 1.9 copy.112
  (96 shorter events, 11.0 us)
Async XLA Ops:
  7.2 1.7 copy-start
  7.2 160.6 %reduce-scatter.3.cloned.1.call-start = ((), (), s32[]{:S(2)}) async-start(), calls=%async_computation.2 | async-start | bytes 2654208 | tf_op jit(solution)/shard_map/reduce_scatter | solution.py:72
  11.6 7.2 %copy-start.2 = (bf16[1,32,96,256]{3,2,1,0:T(8,128)(2,1)S(1)}, bf16[1,32,96,256]{3,2,1,0:T(8,128)(2,1)}, u32[]{:S(2)}) copy-start(bf16[1,32,96,256]{3,2,1,0:T(8,128)(2,1)} %param.17) | copy-start | bytes 4718596
  15.6 47.5 %collective-permute-start = (f32[17,256]{1,0:T(8,128)}, f32[17,256]{1,0:T(8,128)}, u32[]{:S(2)}, u32[]{:S(2)}) collective-permute-start(f32[17,256]{1,0:T(8,128)} %bitcast.133), channel_id=1, source_target_pairs={{1,0},{2,1},{3,2},{5,4},{6,5},{7,6},{9,8},{10,9},{11,10},{13,12},{... | collective-permute-start | bytes 52232 | tf_op jit(solution)/shard_map/ppermute | solution.py:11
  17.5 78.1 %collective-permute-start.1 = (f32[48,256]{1,0:T(8,128)}, f32[48,256]{1,0:T(8,128)}, u32[]{:S(2)}, u32[]{:S(2)}) collective-permute-start(f32[48,256]{1,0:T(8,128)} %slice_bitcast_fusion.13), channel_id=1, source_target_pairs={{4,0},{5,1},{6,2},{7,3},{12,8},{13,9},{14,10},{15,11},{20,16},{21,... | collective-permute-start | bytes 147464 | tf_op jit(solution)/shard_map/ppermute | solution.py:11
  19.5 18.7 %collective-permute-start.6 = (bf16[32,256]{1,0:T(8,128)(2,1)}, bf16[32,256]{1,0:T(8,128)(2,1)}, u32[]{:S(2)}, u32[]{:S(2)}) collective-permute-start(bf16[32,256]{1,0:T(8,128)(2,1)} %bitcast.134), channel_id=1, source_target_pairs={{0,1},{1,2},{2,3},{4,5},{5,6},{6,7},{8,9},{9,10},{10,11},{12,13},{... | collective-permute-start | bytes 49160 | tf_op jit(solution)/shard_map/ppermute | solution.py:11
  26.2 40.3 %collective-permute-start.8 = (bf16[96,256]{1,0:T(8,128)(2,1)}, bf16[96,256]{1,0:T(8,128)(2,1)}, u32[]{:S(2)}, u32[]{:S(2)}) collective-permute-start(bf16[96,256]{1,0:T(8,128)(2,1)} %slice_bitcast_fusion.14), channel_id=1, source_target_pairs={{0,4},{1,5},{2,6},{3,7},{8,12},{9,13},{10,14},{11,15},{16,20},{17,... | collective-permute-start | bytes 147464 | tf_op jit(solution)/shard_map/ppermute | solution.py:11
  39.0 0.6 copy-start.8
  61.2 5.3 %collective-permute-start.7 = (bf16[1,256]{1,0:T(2,128)(2,1)}, bf16[1,256]{1,0:T(2,128)(2,1)}, u32[]{:S(2)}, u32[]{:S(2)}) collective-permute-start(bf16[1,256]{1,0:T(2,128)(2,1)} %slice.361), channel_id=1, source_target_pairs={{0,4},{1,5},{2,6},{3,7},{8,12},{9,13},{10,14},{11,15},{16,20},{17,... | collective-permute-start | bytes 1544 | tf_op jit(solution)/shard_map/ppermute | solution.py:11
  65.1 30.5 %collective-permute-start.2 = (f32[1,256]{1,0:T(1,128)}, f32[1,256]{1,0:T(1,128)}, u32[]{:S(2)}, u32[]{:S(2)}) collective-permute-start(f32[1,256]{1,0:T(1,128)} %slice.345), channel_id=1, source_target_pairs={{4,0},{5,1},{6,2},{7,3},{12,8},{13,9},{14,10},{15,11},{20,16},{21,... | collective-permute-start | bytes 3080 | tf_op jit(solution)/shard_map/ppermute | solution.py:11
  70.4 30.7 %copy-start.6 = (bf16[16,48,256]{2,1,0:T(8,128)(2,1)S(1)}, bf16[16,48,256]{2,1,0:T(8,128)(2,1)}, u32[]{:S(2)}) copy-start(bf16[16,48,256]{2,1,0:T(8,128)(2,1)} %slice.314) | copy-start | bytes 1179652
  78.0 23.9 %copy-start.4 = (bf16[16,48,256]{2,1,0:T(8,128)(2,1)S(1)}, bf16[16,48,256]{2,1,0:T(8,128)(2,1)}, u32[]{:S(2)}) copy-start(bf16[16,48,256]{2,1,0:T(8,128)(2,1)} %slice.315) | copy-start | bytes 1179652
  88.0 15.6 %copy-start.5 = (bf16[16,48,256]{2,1,0:T(8,128)(2,1)S(1)}, bf16[16,48,256]{2,1,0:T(8,128)(2,1)}, u32[]{:S(2)}) copy-start(bf16[16,48,256]{2,1,0:T(8,128)(2,1)} %slice.317) | copy-start | bytes 1179652
  101.1 5.0 %copy-start.3 = (bf16[1,16,48,256]{3,2,1,0:T(8,128)(2,1)S(1)}, bf16[1,16,48,256]{3,2,1,0:T(8,128)(2,1)}, u32[]{:S(2)}) copy-start(bf16[1,16,48,256]{3,2,1,0:T(8,128)(2,1)} %param.18) | copy-start | bytes 1179652
  110.7 157.4 %reduce-scatter.5.cloned.1.call-start = ((), (), s32[]{:S(2)}) async-start(), calls=%async_computation.3 | async-start | bytes 5308416 | tf_op jit(solution)/shard_map/reduce_scatter | solution.py:72
  110.8 8.2 %collective-permute-start.9 = (bf16[16,256]{1,0:T(8,128)(2,1)S(1)}, bf16[16,256]{1,0:T(8,128)(2,1)S(1)}, u32[]{:S(2)}, u32[]{:S(2)}) collective-permute-start(bf16[16,256]{1,0:T(8,128)(2,1)S(1)} %bitcast.150), channel_id=1, source_target_pairs={{0,1},{1,2},{2,3},{4,5},{5,6},{6,7},{8,9},{9,10},{10,11},{12,13},{... | collective-permute-start | bytes 24584 | tf_op jit(solution)/shard_map/ppermute | solution.py:11
  114.2 7.0 %collective-permute-start.11 = (bf16[48,256]{1,0:T(8,128)(2,1)S(1)}, bf16[48,256]{1,0:T(8,128)(2,1)S(1)}, u32[]{:S(2)}, u32[]{:S(2)}) collective-permute-start(bf16[48,256]{1,0:T(8,128)(2,1)S(1)} %slice_bitcast_fusion.16), channel_id=1, source_target_pairs={{0,4},{1,5},{2,6},{3,7},{8,12},{9,13},{10,14},{11,15},{16,20},{17,... | collective-permute-start | bytes 73736 | tf_op jit(solution)/shard_map/ppermute | solution.py:11
  118.1 4.3 %copy-start.9 = (bf16[1,8,24,512]{3,2,1,0:T(8,128)(2,1)S(1)}, bf16[1,8,24,512]{3,2,1,0:T(8,128)(2,1)}, u32[]{:S(2)}) copy-start(bf16[1,8,24,512]{3,2,1,0:T(8,128)(2,1)} %param.19) | copy-start | bytes 589828
  119.0 2.1 collective-permute-start.10
  125.4 1.3 copy-start.7
  125.4 196.2 %all-reduce.15.cloned.1.call-start = ((), (), s32[]{:S(2)}) async-start(), calls=%async_computation.4 | async-start | bytes 1769472 | tf_op jit(solution)/shard_map/psum | solution.py:65
  138.8 8.1 %collective-permute-start.3 = (f32[33,256]{1,0:T(8,128)S(1)}, f32[33,256]{1,0:T(8,128)S(1)}, u32[]{:S(2)}, u32[]{:S(2)}) collective-permute-start(f32[33,256]{1,0:T(8,128)S(1)} %bitcast.148), channel_id=1, source_target_pairs={{1,0},{2,1},{3,2},{5,4},{6,5},{7,6},{9,8},{10,9},{11,10},{13,12},{... | collective-permute-start | bytes 101384 | tf_op jit(solution)/shard_map/ppermute | solution.py:11
  142.9 127.8 %collective-permute-start.4 = (f32[96,256]{1,0:T(8,128)}, f32[96,256]{1,0:T(8,128)S(1)}, u32[]{:S(2)}, u32[]{:S(2)}) collective-permute-start(f32[96,256]{1,0:T(8,128)} %slice_bitcast_fusion.12), channel_id=1, source_target_pairs={{4,0},{5,1},{6,2},{7,3},{12,8},{13,9},{14,10},{15,11},{20,16},{21,... | collective-permute-start | bytes 294920 | tf_op jit(solution)/shard_map/ppermute | solution.py:11
  146.9 0.6 copy-start.10
  147.6 123.1 %collective-permute-start.5 = (f32[1,256]{1,0:T(1,128)S(1)}, f32[1,256]{1,0:T(1,128)S(1)}, u32[]{:S(2)}, u32[]{:S(2)}) collective-permute-start(f32[1,256]{1,0:T(1,128)S(1)} %slice.359), channel_id=1, source_target_pairs={{4,0},{5,1},{6,2},{7,3},{12,8},{13,9},{14,10},{15,11},{20,16},{21,... | collective-permute-start | bytes 3080 | tf_op jit(solution)/shard_map/ppermute | solution.py:11
  270.7 54.5 %copy-start.1 = (bf16[3,3,256,512]{3,2,1,0:T(8,128)(2,1)S(1)}, bf16[3,3,256,512]{3,2,1,0:T(8,128)(2,1)}, u32[]{:S(2)}) copy-start(bf16[3,3,256,512]{3,2,1,0:T(8,128)(2,1)} %param.21) | copy-start | bytes 7077892
Sparse Core Ops, SparseCore 0:
  110.8 56.8 reduce-scatter.2
  170.0 97.9 reduce-scatter.4
  271.2 50.3 all-reduce.14
where the time goes:
time: 335 us; the launch traced here: 332 us
  waiting for transfers between devices  168 us (50%)
  local copies, waits for them, and re-layouts  94.8 us (28%)
  starting transfers between devices  27.9 us (8%)
  other arithmetic  16.2 us (5%)
  between operations  14.4 us (4%)
  matrix products  10.6 us (3%)
    reduce_scatter x2, waiting for transfers between devices, kernel_gradient(): lax.psum_scatter(slide_sums, ('row', 'col'), scatter_dimension=0, tiled=T...  119 us
    slice x18, local copies, waits for them, and re-layouts, gather_taps(): extended[tap_row:tap_row + 2 * out_rows:2, tap_col:tap_col + 2 * out_cols:2]  53.5 us
    psum x1, waiting for transfers between devices, kernel_gradient(): lax.psum(lax.dot_general(patches, gradient, (((0,), (0,)), ((), ())), pre...  45.9 us
    ppermute x12, starting transfers between devices, shifted(): return lax.ppermute(value, axis, pairs)  27.6 us
    unnamed x44, local copies, waits for them, and re-layouts  16.4 us
    dot_general x2, matrix products, kernel_gradient(): lax.dot_general(patches, gradient, (((0,), (0,)), ((), ())), preferred_el...  7.61 us
  transfers between devices with their start and end apart: 15, of which 4 were waited for; matrix products, arithmetic and copies ran while one was open for 28% of the time, Pallas kernels for 0%

commit v1 on v0

--- a/solution.py
+++ b/solution.py
@@ -62,12 +62,15 @@
 
 
 def kernel_gradient(patches, gradient, norm_scale):
-    slide_sums = lax.psum(
-        lax.dot_general(
-            patches, gradient, (((0,), (0,)), ((), ())), preferred_element_type=jnp.float32
-        )
-        * norm_scale,
-        "dp",
+    slide_sums = jnp.sum(
+        lax.all_gather(
+            lax.dot_general(
+                patches, gradient, (((0,), (0,)), ((), ())), preferred_element_type=jnp.float32
+            )
+            * norm_scale,
+            "dp",
+        ),
+        axis=0,
     )
     return lax.psum_scatter(slide_sums, ("row", "col"), scatter_dimension=0, tiled=True)
 

time: 335 us -> 559 us (1.67)
  waiting for transfers between devices: 168 us -> 371 us
  other arithmetic: 16.2 us -> 32 us
  local copies, waits for them, and re-layouts: 94.8 us -> 101 us
    all_gather x0 -> x2, waiting for transfers between devices: none -> 256 us  [kernel_gradient(): lax.all_gather(lax.dot_general(patches, gradient, (((0,), (0,)), ((), ())...]
    psum x1 -> x0, waiting for transfers between devices: 45.9 us -> none  [kernel_gradient(): lax.psum(lax.dot_general(patches, gradient, (((0,), (0,)), ((), ())), pre...]
    reduce_sum x0 -> x2, other arithmetic: none -> 17.5 us  [kernel_gradient(): jnp.sum(lax.all_gather(lax.dot_general(patches, gradient, (((0,), (0,)),...]
    slice x18, local copies, waits for them, and re-layouts: 53.5 us -> 61.5 us  [gather_taps(): extended[tap_row:tap_row + 2 * out_rows:2, tap_col:tap_col + 2 * out_cols:2]]
    unnamed x44 -> x42, local copies, waits for them, and re-layouts: 16.4 us -> 9.11 us
  transfers between devices with their start and end apart: 15 -> 16, of which waited for: 4 -> 4; matrix products, arithmetic and copies ran while one was open for 28% -> 23% of each run, Pallas kernels for 0% -> 0%
where the time goes in v1:
time: 559 us; the launch traced here: 556 us
  waiting for transfers between devices  371 us (66%)
  local copies, waits for them, and re-layouts  101 us (18%)
  other arithmetic  32 us (6%)
  starting transfers between devices  27.2 us (5%)
  between operations  14.5 us (3%)
  matrix products  10.7 us (2%)
    all_gather x2, waiting for transfers between devices, kernel_gradient(): lax.all_gather(lax.dot_general(patches, gradient, (((0,), (0,)), ((), ())...  256 us
    reduce_scatter x2, waiting for transfers between devices, kernel_gradient(): lax.psum_scatter(slide_sums, ('row', 'col'), scatter_dimension=0, tiled=T...  115 us
    slice x18, local copies, waits for them, and re-layouts, gather_taps(): extended[tap_row:tap_row + 2 * out_rows:2, tap_col:tap_col + 2 * out_cols:2]  61.5 us
    ppermute x12, starting transfers between devices, shifted(): return lax.ppermute(value, axis, pairs)  26.9 us
    reduce_sum x2, other arithmetic, kernel_gradient(): jnp.sum(lax.all_gather(lax.dot_general(patches, gradient, (((0,), (0,)),...  17.5 us
  transfers between devices with their start and end apart: 16, of which 4 were waited for; matrix products, arithmetic and copies ran while one was open for 23% of the time, Pallas kernels for 0%

profile of v1, /device:TPU:0, one launch (start us, length us, event | category | flops | bytes accessed | tf_op | source)
XLA Modules:
  0.0 556.3 jit_solution(5251457582979202067)
XLA Ops:
  7.2 1.1 slice.360
  8.3 4.9 collective-permute-start.6
  13.3 1.4 slice_bitcast_fusion.14
  14.7 2.1 collective-permute-start.8
  16.8 1.8 fusion.1
  19.5 1.6 copy.44
  21.1 1.8 reshape.226
  23.4 1.3 collective-permute-start
  24.7 0.6 slice_bitcast_fusion.13
  25.4 1.3 collective-permute-start.1
  26.7 5.2 slice.319
  31.9 5.2 slice.318
  37.1 5.2 slice.316
  42.3 5.2 slice.315
  48.1 2.1 pad_maximum_fusion.2
  50.2 7.5 %slice.314 = bf16[16,48,256]{2,1,0:T(8,128)(2,1)S(1)} slice(bf16[32,97,256]{2,1,0:T(8,128)(2,1)} %pad_maximum_fusion.2), slice={[0:32:2], [0:96:2], [0:256:1]} | slice | bytes 786432 | tf_op jit(solution)/shard_map/slice | solution.py:28
  57.8 7.5 %slice.317 = bf16[16,48,256]{2,1,0:T(8,128)(2,1)S(1)} slice(bf16[32,97,256]{2,1,0:T(8,128)(2,1)} %pad_maximum_fusion.2), slice={[1:32:2], [0:96:2], [0:256:1]} | slice | bytes 786432 | tf_op jit(solution)/shard_map/slice | solution.py:28
  65.3 0.7 slice.361
  66.0 3.6 collective-permute-start.7
  69.6 0.7 fusion.10
  70.4 0.7 slice.345
  71.1 1.3 collective-permute-start.2
  72.5 0.8 maximum_bitcast_fusion
  73.3 2.2 maximum_maximum_fusion
  75.5 7.5 %slice.311 = bf16[16,48,256]{2,1,0:T(8,128)(2,1)S(1)} slice(bf16[33,97,256]{2,1,0:T(8,128)(2,1)} %maximum_maximum_fusion), slice={[0:32:2], [0:96:2], [0:256:1]} | slice | bytes 786432 | tf_op jit(solution)/shard_map/slice | solution.py:28
  83.1 0.8 constant_dynamic-update-slice_fusion.8
  83.9 7.6 %slice.313 = bf16[16,48,256]{2,1,0:T(8,128)(2,1)S(1)} slice(bf16[33,97,256]{2,1,0:T(8,128)(2,1)} %maximum_maximum_fusion), slice={[0:32:2], [2:97:2], [0:256:1]} | slice | bytes 786432 | tf_op jit(solution)/shard_map/slice | solution.py:28
  91.5 7.5 %slice.312 = bf16[16,48,256]{2,1,0:T(8,128)(2,1)S(1)} slice(bf16[33,97,256]{2,1,0:T(8,128)(2,1)} %maximum_maximum_fusion), slice={[0:32:2], [1:97:2], [0:256:1]} | slice | bytes 786432 | tf_op jit(solution)/shard_map/slice | solution.py:28
  99.1 0.7 fusion.12
  99.9 1.3 scatter-add.21
  101.2 0.8 fusion.8
  102.0 0.8 constant_dynamic-update-slice_fusion.7
  102.8 0.8 constant_dynamic-update-slice_fusion.6
  103.6 0.9 constant_dynamic-update-slice_fusion.5
  104.4 0.8 constant_dynamic-update-slice_fusion.4
  105.3 0.8 constant_dynamic-update-slice_fusion.3
  106.1 0.8 constant_dynamic-update-slice_fusion.2
  107.0 0.8 constant_dynamic-update-slice_fusion.1
  107.8 0.8 constant_dynamic-update-slice_fusion
  108.6 4.5 fusion
  113.3 4.5 collective-permute-start.9
  117.9 2.7 collective-permute-start.11
  122.1 1.3 collective-permute-start.10
  125.5 3.1 convolution_multiply_fusion
  128.7 84.6 %all-gather.5.cloned.1.call-done = f32[9216,256]{1,0:T(8,128)} async-done(((f32[2304,256]{1,0:T(8,128)}), f32[9216,256]{1,0:T(8,128)}) %all-gather.5.cloned.1.call-update) | async-done | bytes 9437200 | tf_op jit(solution)/shard_map/all_gather | solution.py:66
  213.3 6.0 %reduce_sum.18 = f32[2304,256]{1,0:T(8,128)} reduce(f32[4,2304,256]{2,1,0:T(8,128)} %bitcast.147, f32[]{:T(128)} %constant.173.clone.1), dimensions={0}, to_apply=%region_0.1 | reduce | flops 1769472 | bytes 11796484 | tf_op jit(solution)/shard_map/reduce_sum | solution.py:65
  219.6 171.6 %all-gather.7.cloned.1.call-done = f32[9216,512]{1,0:T(8,128)} async-done(((f32[2304,512]{1,0:T(8,128)}), f32[9216,512]{1,0:T(8,128)}) %all-gather.7.cloned.1.call-update) | async-done | bytes 18874384 | tf_op jit(solution)/shard_map/all_gather | solution.py:66
  391.2 11.5 %reduce_sum.19 = f32[2304,512]{1,0:T(8,128)} reduce(f32[4,2304,512]{2,1,0:T(8,128)} %bitcast.139, f32[]{:T(128)} %constant.173.clone.1), dimensions={0}, to_apply=%region_2.3 | reduce | flops 3538944 | bytes 23592964 | tf_op jit(solution)/shard_map/reduce_sum | solution.py:65
  402.7 1.2 copy-done.8
  403.9 1.1 fusion.3
  408.3 3.4 copy.53
  411.7 5.5 reshape.231
  417.2 1.0 slice.354
  418.2 1.3 collective-permute-start.3
  419.5 0.9 slice_bitcast_fusion.12
  420.4 1.0 slice.353
  421.3 4.1 slice.352
  425.4 1.3 collective-permute-start.4
  426.7 1.3 collective-permute-start.5
  428.1 1.8 scatter-add.25
  430.0 1.7 fusion.7
  431.6 3.3 convert_bitcast_fusion
  434.9 14.1 %reduce-scatter.3.cloned.1.call-done = f32[288,256]{1,0:T(8,128)} async-done(((f32[2304,256]{1,0:T(8,128)}), f32[288,256]{1,0:T(8,128)}) %reduce-scatter.3.cloned.1.call-update) | async-done | bytes 294928 | tf_op jit(solution)/shard_map/reduce_scatter | solution.py:75
  449.0 100.7 %reduce-scatter.5.cloned.1.call-done = f32[288,512]{1,0:T(8,128)} async-done(((f32[2304,512]{1,0:T(8,128)}), f32[288,512]{1,0:T(8,128)}) %reduce-scatter.5.cloned.1.call-update) | async-done | bytes 589840 | tf_op jit(solution)/shard_map/reduce_scatter | solution.py:75
  (99 shorter events, 9.4 us)
Async XLA Ops:
  7.2 9.6 %copy-start = (bf16[3,3,256,512]{3,2,1,0:T(8,128)(2,1)S(1)}, bf16[3,3,256,512]{3,2,1,0:T(8,128)(2,1)}, u32[]{:S(2)}) copy-start(bf16[3,3,256,512]{3,2,1,0:T(8,128)(2,1)} %param.21) | copy-start | bytes 7077892
  7.2 206.1 %all-gather.5.cloned.1.call-start = ((), (), s32[]{:S(2)}) async-start(), calls=%async_computation.4 | async-start | bytes 11796480 | tf_op jit(solution)/shard_map/all_gather | solution.py:66
  8.3 39.2 %collective-permute-start.6 = (bf16[32,256]{1,0:T(8,128)(2,1)S(1)}, bf16[32,256]{1,0:T(8,128)(2,1)S(1)}, u32[]{:S(2)}, u32[]{:S(2)}) collective-permute-start(bf16[32,256]{1,0:T(8,128)(2,1)S(1)} %bitcast.154), channel_id=1, source_target_pairs={{0,1},{1,2},{2,3},{4,5},{5,6},{6,7},{8,9},{9,10},{10,11},{12,13},{... | collective-permute-start | bytes 49160 | tf_op jit(solution)/shard_map/ppermute | solution.py:11
  14.7 57.8 %collective-permute-start.8 = (bf16[96,256]{1,0:T(8,128)(2,1)}, bf16[96,256]{1,0:T(8,128)(2,1)}, u32[]{:S(2)}, u32[]{:S(2)}) collective-permute-start(bf16[96,256]{1,0:T(8,128)(2,1)} %slice_bitcast_fusion.14), channel_id=1, source_target_pairs={{0,4},{1,5},{2,6},{3,7},{8,12},{9,13},{10,14},{11,15},{16,20},{17,... | collective-permute-start | bytes 147464 | tf_op jit(solution)/shard_map/ppermute | solution.py:11
  19.5 7.2 %copy-start.2 = (bf16[1,32,96,256]{3,2,1,0:T(8,128)(2,1)S(1)}, bf16[1,32,96,256]{3,2,1,0:T(8,128)(2,1)}, u32[]{:S(2)}) copy-start(bf16[1,32,96,256]{3,2,1,0:T(8,128)(2,1)} %param.17) | copy-start | bytes 4718596
  23.4 46.1 %collective-permute-start = (f32[17,256]{1,0:T(8,128)}, f32[17,256]{1,0:T(8,128)}, u32[]{:S(2)}, u32[]{:S(2)}) collective-permute-start(f32[17,256]{1,0:T(8,128)} %bitcast.135), channel_id=1, source_target_pairs={{1,0},{2,1},{3,2},{5,4},{6,5},{7,6},{9,8},{10,9},{11,10},{13,12},{... | collective-permute-start | bytes 52232 | tf_op jit(solution)/shard_map/ppermute | solution.py:11
  25.4 73.7 %collective-permute-start.1 = (f32[48,256]{1,0:T(8,128)}, f32[48,256]{1,0:T(8,128)}, u32[]{:S(2)}, u32[]{:S(2)}) collective-permute-start(f32[48,256]{1,0:T(8,128)} %slice_bitcast_fusion.13), channel_id=1, source_target_pairs={{4,0},{5,1},{6,2},{7,3},{12,8},{13,9},{14,10},{15,11},{20,16},{21,... | collective-permute-start | bytes 147464 | tf_op jit(solution)/shard_map/ppermute | solution.py:11
  47.5 0.6 copy-start.10
  66.0 6.5 %collective-permute-start.7 = (bf16[1,256]{1,0:T(2,128)(2,1)S(1)}, bf16[1,256]{1,0:T(2,128)(2,1)S(1)}, u32[]{:S(2)}, u32[]{:S(2)}) collective-permute-start(bf16[1,256]{1,0:T(2,128)(2,1)S(1)} %slice.361), channel_id=1, source_target_pairs={{0,4},{1,5},{2,6},{3,7},{8,12},{9,13},{10,14},{11,15},{16,20},{17,... | collective-permute-start | bytes 1544 | tf_op jit(solution)/shard_map/ppermute | solution.py:11
  71.1 28.0 %collective-permute-start.2 = (f32[1,256]{1,0:T(1,128)S(1)}, f32[1,256]{1,0:T(1,128)S(1)}, u32[]{:S(2)}, u32[]{:S(2)}) collective-permute-start(f32[1,256]{1,0:T(1,128)S(1)} %slice.345), channel_id=1, source_target_pairs={{4,0},{5,1},{6,2},{7,3},{12,8},{13,9},{14,10},{15,11},{20,16},{21,... | collective-permute-start | bytes 3080 | tf_op jit(solution)/shard_map/ppermute | solution.py:11
  83.1 21.4 %copy-start.7 = (bf16[16,48,256]{2,1,0:T(8,128)(2,1)S(1)}, bf16[16,48,256]{2,1,0:T(8,128)(2,1)}, u32[]{:S(2)}) copy-start(bf16[16,48,256]{2,1,0:T(8,128)(2,1)} %slice.315) | copy-start | bytes 1179652
  83.9 21.4 %copy-start.6 = (bf16[16,48,256]{2,1,0:T(8,128)(2,1)S(1)}, bf16[16,48,256]{2,1,0:T(8,128)(2,1)}, u32[]{:S(2)}) copy-start(bf16[16,48,256]{2,1,0:T(8,128)(2,1)} %slice.316) | copy-start | bytes 1179652
  99.1 7.9 %copy-start.5 = (bf16[16,48,256]{2,1,0:T(8,128)(2,1)S(1)}, bf16[16,48,256]{2,1,0:T(8,128)(2,1)}, u32[]{:S(2)}) copy-start(bf16[16,48,256]{2,1,0:T(8,128)(2,1)} %slice.318) | copy-start | bytes 1179652
  102.8 5.0 copy-start.4
  103.6 5.0 copy-start.3
  113.1 278.0 %all-gather.7.cloned.1.call-start = ((), (), s32[]{:S(2)}) async-start(), calls=%async_computation.5 | async-start | bytes 23592960 | tf_op jit(solution)/shard_map/all_gather | solution.py:66
  113.3 8.8 %collective-permute-start.9 = (bf16[16,256]{1,0:T(8,128)(2,1)S(1)}, bf16[16,256]{1,0:T(8,128)(2,1)S(1)}, u32[]{:S(2)}, u32[]{:S(2)}) collective-permute-start(bf16[16,256]{1,0:T(8,128)(2,1)S(1)} %bitcast.156), channel_id=1, source_target_pairs={{0,1},{1,2},{2,3},{4,5},{5,6},{6,7},{8,9},{9,10},{10,11},{12,13},{... | collective-permute-start | bytes 24584 | tf_op jit(solution)/shard_map/ppermute | solution.py:11
  117.9 6.4 %collective-permute-start.11 = (bf16[48,256]{1,0:T(8,128)(2,1)S(1)}, bf16[48,256]{1,0:T(8,128)(2,1)S(1)}, u32[]{:S(2)}, u32[]{:S(2)}) collective-permute-start(bf16[48,256]{1,0:T(8,128)(2,1)S(1)} %slice_bitcast_fusion.16), channel_id=1, source_target_pairs={{0,4},{1,5},{2,6},{3,7},{8,12},{9,13},{10,14},{11,15},{16,20},{17,... | collective-permute-start | bytes 73736 | tf_op jit(solution)/shard_map/ppermute | solution.py:11
  121.6 3.9 copy-start.9
  122.1 2.1 collective-permute-start.10
  128.7 320.3 %reduce-scatter.3.cloned.1.call-start = ((), (), s32[]{:S(2)}) async-start(), calls=%async_computation.2 | async-start | bytes 2654208 | tf_op jit(solution)/shard_map/reduce_scatter | solution.py:75
  219.4 330.4 %reduce-scatter.5.cloned.1.call-start = ((), (), s32[]{:S(2)}) async-start(), calls=%async_computation.3 | async-start | bytes 5308416 | tf_op jit(solution)/shard_map/reduce_scatter | solution.py:75
  402.7 1.3 copy-start.8
  418.2 8.6 %collective-permute-start.3 = (f32[33,256]{1,0:T(8,128)S(1)}, f32[33,256]{1,0:T(8,128)S(1)}, u32[]{:S(2)}, u32[]{:S(2)}) collective-permute-start(f32[33,256]{1,0:T(8,128)S(1)} %bitcast.152), channel_id=1, source_target_pairs={{1,0},{2,1},{3,2},{5,4},{6,5},{7,6},{9,8},{10,9},{11,10},{13,12},{... | collective-permute-start | bytes 101384 | tf_op jit(solution)/shard_map/ppermute | solution.py:11
  425.4 4.5 collective-permute-start.4
  426.7 3.2 collective-permute-start.5
  429.9 119.8 %copy-start.1 = (bf16[3,3,256,512]{3,2,1,0:T(8,128)(2,1)S(1)}, bf16[3,3,256,512]{3,2,1,0:T(8,128)(2,1)}, u32[]{:S(2)}) copy-start(bf16[3,3,256,512]{3,2,1,0:T(8,128)(2,1)} %param.21) | copy-start | bytes 7077892
Sparse Core Ops, SparseCore 0:
  113.3 100.0 all-gather.4
  215.2 175.9 all-gather.6
  394.1 54.8 reduce-scatter.2
  451.7 97.9 reduce-scatter.4
